TPU v7x, 32 devices: a whole 2x2x4 slice. The times are simulated.
32 devices in a mesh: tm: 8 (over y, x, core), tile: 4 (over z).
Axes of the slice: x: 2, y: 2, z: 4, core: 2. Of those that a mesh axis runs over, the one named last changes fastest.
Arguments:
- velocity_u: float32 [384, 2, 16, 1024], P('tm', None, None, 'tile'), may hold values from -12 to 12
- velocity_v: float32 [384, 2, 16, 1024], P('tm', None, None, 'tile'), may hold values from -12 to 12
- land_sea: int32 [16, 1024], P(None, 'tile'), may hold values 0 or 1
- bottom_level: int32 [16, 1024], P(None, 'tile'), may hold values from 0 to 2
- spacing_x: float32 [16, 1024], P(None, 'tile'), may hold values from 0.5 to 2
- spacing_y: float32 [16, 1024], P(None, 'tile'), may hold values from 0.5 to 2
Outputs:
- conversion_maps: bfloat16 [384, 2, 16, 1024], P('tm', None, None, 'tile')
- mean_map: float32 [2, 16, 1024], P(None, None, 'tile')
All inputs are finite; a program needn't handle non-finite values. No bound on the sum of `land_sea` on one device may be relied on, other than what follows from the above.
Results may differ from a plain program's by a relative error of at most 0.001.
Values sent between devices are 32-bit elements; how exact they have to be, the bound alone decides.
A program may use at most 64 MiB of HBM per device.

v0:
```python
import jax
import jax.numpy as jnp
from jax import lax
from jax.sharding import PartitionSpec as P

HALF = 24
SNAPS = 48
cutoff_freq = 1.0 / 40.0


def extended(x, sides, width):
    for axis, dim in sides:
        size, length = (lax.axis_size(axis), x.shape[dim])
        up = [(i, (i + 1) % size) for i in range(size - 1)]
        down = [(j, i) for i, j in up]
        last = lax.slice_in_dim(x, length - width, length, axis=dim)
        first = lax.slice_in_dim(x, 0, width, axis=dim)
        before = lax.ppermute(last, axis, up)
        after = lax.ppermute(first, axis, down)
        x = jnp.concatenate([before, x, after], axis=dim)
    return x


def band_matrix(count):
    out_rows = jnp.arange(count, dtype=jnp.int32)[:, None]
    in_cols = jnp.arange(count + 2 * HALF, dtype=jnp.int32)[None, :]
    offset = (in_cols - out_rows - HALF).astype(jnp.float32)
    weights = 2.0 * cutoff_freq * jnp.sinc(2.0 * cutoff_freq * offset) * jnp.sinc(offset / HALF)
    return jnp.where(jnp.abs(offset) <= HALF, weights, jnp.zeros_like(weights))


def lowpass(padded, validity, blocks, block):
    matrix = band_matrix(block)

    def one_block(block_id):
        start = block_id * block
        window = lax.dynamic_slice_in_dim(padded, start, block + 2 * HALF, 0)
        valid_part = lax.dynamic_slice_in_dim(validity, start, block + 2 * HALF, 0)
        weighted = jnp.dot(
            matrix, window, precision=lax.Precision.HIGHEST, preferred_element_type=jnp.float32
        )
        weight_sum = jnp.dot(
            matrix, valid_part, precision=lax.Precision.HIGHEST, preferred_element_type=jnp.float32
        )
        return weighted / weight_sum[:, None]

    result = lax.map(one_block, jnp.arange(blocks, dtype=jnp.int32))
    return result.reshape(blocks * block, padded.shape[1])


def wet_cells(land_sea, bottom_level, levels):
    level_ids = jnp.arange(levels, dtype=jnp.int32)[:, None, None]
    return ((land_sea[None] == 1) & (level_ids < bottom_level[None])).astype(jnp.float32)


def filter_series(series):
    length = series.shape[0]
    flattened = series.reshape(length, -1)
    padded = jnp.pad(flattened, ((HALF, HALF), (0, 0)))
    validity = jnp.pad(jnp.ones((length,), jnp.float32), (HALF, HALF))
    return lowpass(padded, validity, length // SNAPS, SNAPS).reshape(series.shape)


def shards(velocity_u, velocity_v, land_sea, bottom_level, spacing_x, spacing_y):
    block_len = velocity_u.shape[0]
    total_len = block_len * lax.axis_size("tm")
    stacked = jnp.stack([velocity_u, velocity_v], axis=1)
    full_shape = stacked.shape
    flat_cells = stacked.reshape(block_len, 2, -1)
    series_mean = filter_series(
        lax.all_to_all(flat_cells, "tm", split_axis=2, concat_axis=0, tiled=True)
    )
    mean_flat = lax.all_to_all(series_mean, "tm", split_axis=0, concat_axis=2, tiled=True)
    mean_flow = mean_flat.reshape(full_shape)
    eddies = stacked - mean_flow
    wet_mask = wet_cells(land_sea, bottom_level, full_shape[2])
    masked = mean_flow * wet_mask[None, None]
    edge_cols = jnp.concatenate([masked[..., :1], masked[..., -1:]], axis=4)
    edge_ext = extended(edge_cols, (("tile", 4),), 1)
    left_col = edge_ext[..., :1]
    right_col = edge_ext[..., 3:4]
    ahead = jnp.concatenate([masked[..., 1:], right_col], axis=4)
    behind = jnp.concatenate([left_col, masked[..., :-1]], axis=4)
    grad_x = (ahead - behind) * (0.5 / spacing_x)
    row_padded = jnp.pad(masked, ((0, 0), (0, 0), (0, 0), (1, 1), (0, 0)))
    grad_y = (row_padded[..., 2:, :] - row_padded[..., :-2, :]) * (0.5 / spacing_y)
    eddy_u = eddies[:, 0]
    eddy_v = eddies[:, 1]
    total = (
        eddy_u * eddy_u * grad_x[:, 0]
        + eddy_u * eddy_v * (grad_y[:, 0] + grad_x[:, 1])
        + eddy_v * eddy_v * grad_y[:, 1]
    )
    conversion = -wet_mask[None] * total
    summed = lax.psum(jnp.sum(conversion, axis=0), "tm")
    return (conversion.astype(jnp.bfloat16), summed / total_len)


def solution(mesh):
    in_specs = (
        P("tm", None, None, "tile"),
        P("tm", None, None, "tile"),
        P(None, "tile"),
        P(None, "tile"),
        P(None, "tile"),
        P(None, "tile"),
    )
    out_specs = (P("tm", None, None, "tile"), P(None, None, "tile"))
    return jax.shard_map(shards, mesh=mesh, in_specs=in_specs, out_specs=out_specs, check_vma=False)
```

profile of v0, /device:TPU:0, one launch (start us, length us, event | category | flops | bytes accessed | tf_op | source)
XLA Modules:
  0.0 262.7 jit_solution(6098952019784487532)
XLA Ops:
  0.6 2.7 %stack.18 = f32[48,1,8192]{2,0,1:T(8,128)} reshape(f32[48,2,16,256]{3,2,1,0:T(8,128)} %param.9) | data formatting | bytes 3145728 | tf_op jit(solution)/shard_map/stack | solution.py:67
  3.3 1.4 stack.19
  4.8 2.1 pad_maximum_fusion
  6.9 8.0 %copy.21 = f32[48,2,8192]{0,1,2:T(2,128)} copy(f32[48,2,8192]{2,0,1:T(8,128)S(1)} %pad_maximum_fusion) | data formatting | bytes 6291456 | tf_op jit(solution)/shard_map/stack | solution.py:67
  14.9 16.2 %reshape.50 = f32[8,1,98304]{2,1,0:T(1,128)} reshape(f32[8192,2,48]{2,1,0:T(2,128)} %bitcast.49) | data formatting | bytes 6291456
  31.0 5.4 %all-to-all-start = ((f32[8,1,98304]{2,1,0:T(1,128)}), f32[8,1,98304]{2,1,0:T(1,128)S(1)}, u32[]{:S(2)}, u32[]{:S(2)}) async-start(f32[8,1,98304]{2,1,0:T(1,128)} %reshape.50), calls=%async_computation | async-start | bytes 6291456 | tf_op jit(solution)/shard_map/all_to_all | solution.py:71
  37.2 36.8 %all-to-all-done = f32[8,1,98304]{2,1,0:T(1,128)S(1)} async-done(((f32[8,1,98304]{2,1,0:T(1,128)}), f32[8,1,98304]{2,1,0:T(1,128)S(1)}, u32[]{:S(2)}, u32[]{:S(2)}) %all-to-all-start) | async-done | bytes 3145760 | tf_op jit(solution)/shard_map/all_to_all | solution.py:71
  74.6 11.2 %reduce = f32[8,98304]{1,0:T(8,128)} reduce(f32[8,1,98304]{2,1,0:T(1,128)S(1)} %all-to-all-done, f32[]{:T(128)} %broadcast.65), dimensions={1}, to_apply=%all_to_all.22.reduce_sub_computation | reduce | bytes 6291460 | tf_op jit(solution)/shard_map/all_to_all | solution.py:71
  85.8 19.3 %reshape.51 = f32[8192,2,48]{2,1,0:T(2,128)} reshape(f32[8,98304]{1,0:T(8,128)} %reduce) | data formatting | bytes 6291456
  105.1 7.0 %copy.30 = f32[48,2,8,1024]{3,2,0,1:T(8,128)S(1)} copy(f32[48,2,8,1024]{0,1,3,2:T(2,128)} %bitcast.50) | data formatting | bytes 6291456 | tf_op jit(solution)/shard_map/all_to_all | solution.py:71
  112.1 2.4 copy.23
  114.5 1.4 copy.31
  116.3 34.3 %while.11 = (s32[]{:T(128)}, f32[8,48,2048]{2,1,0:T(8,128)}, s32[8]{0:T(128)S(1)}, f32[432,2048]{1,0:T(8,128)S(1)}, f32[48,96]{1,0:T(8,128)}, /*index=5*/f32[432...) while((s32[]{:T(128)}, f32[8,48,2048]{2,1,0:T(8,128)}, s32[8]{0:T(128)S(1)}, ...), condition=%wide.region_1.3_spmd.clone, body=%wide.region_0.2_spmd.clone.sunk | while | flops 113399816 | bytes 1224551 | solution.py:47
  117.6 0.9 convolution_bitcast_fusion.2
  118.5 2.1 fusion.59
  121.9 0.9 convolution_bitcast_fusion.2
  122.9 2.1 fusion.59
  126.2 0.9 convolution_bitcast_fusion.2
  127.1 2.1 fusion.59
  130.5 0.9 convolution_bitcast_fusion.2
  131.4 2.1 fusion.59
  134.8 0.9 convolution_bitcast_fusion.2
  135.7 2.1 fusion.59
  139.0 0.9 convolution_bitcast_fusion.2
  140.0 2.1 fusion.59
  143.3 0.9 convolution_bitcast_fusion.2
  144.3 2.1 fusion.59
  147.6 0.9 convolution_bitcast_fusion.2
  148.5 2.1 fusion.59
  150.6 5.6 %reshape_reshape.3 = f32[384,2,1024]{2,1,0:T(2,128)} reshape(f32[8,48,2048]{2,1,0:T(8,128)} %get-tuple-element.38) | data formatting | bytes 6291456 | tf_op jit(solution)/shard_map/reshape;reshape | solution.py:61
  156.2 4.0 %all-to-all-start.1 = ((f32[384,2,1024]{2,1,0:T(2,128)}), f32[384,2,1024]{2,1,0:T(2,128)S(1)}, u32[]{:S(2)}, u32[]{:S(2)}) async-start(f32[384,2,1024]{2,1,0:T(2,128)} %reshape_reshape.3), calls=%async_computation.1 | async-start | bytes 6291456 | tf_op jit(solution)/shard_map/all_to_all | solution.py:73
  160.3 37.7 %all-to-all-done.1 = f32[384,2,1024]{2,1,0:T(2,128)S(1)} async-done(((f32[384,2,1024]{2,1,0:T(2,128)}), f32[384,2,1024]{2,1,0:T(2,128)S(1)}, u32[]{:S(2)}, u32[]{:S(2)}) %all-to-all-start.1) | async-done | bytes 3145760 | tf_op jit(solution)/shard_map/all_to_all | solution.py:73
  198.0 1.0 copy.24
  199.0 1.8 copy.25
  200.8 2.6 reshape.47
  203.4 5.7 %maximum_subtract_fusion = (f32[48,2,2,16,256]{4,3,2,1,0:T(8,128)}, f32[48,2,2,16,256]{4,3,2,1,0:T(8,128)S(1)}) fusion(f32[48,2,2,16,256]{4,3,2,1,0:T(8,128)} %reshape.47, f32[48,1,2,16,256]{4,3,2,1,0:T(8,128)} %bitcast.55, f32[48,1,2,16,256]{4,3,2,1,0:T(8,128)} %bitcast.56, f32[2,16,256]{2,1,0:T(8,128)S(1)} %fusion.15), kind=kLoop, calls=%fused_computation.12 | loop fusion | flops 2359296 | bytes 12615680 | tf_op jit(solution)/shard_map/sub | solution.py:75
  209.1 3.7 %fusion.47 = (f32[48,2,2,16,255]{4,3,2,1,0:T(8,128)}, f32[48,2,2,16,255]{4,3,2,1,0:T(8,128)}) fusion(f32[48,2,2,16,256]{4,3,2,1,0:T(8,128)S(1)} %get-tuple-element.70), kind=kLoop, calls=%fused_computation.85 | loop fusion | bytes 12533760 | tf_op jit(solution)/shard_map/slice | solution.py:83
  212.8 2.3 fusion.46
  215.1 2.2 copy.26
  217.3 1.3 collective-permute-start
  218.6 2.2 copy.28
  220.8 4.7 %collective-permute-start.1 = (f32[48,2,2,16,1]{0,3,4,2,1:T(8,128)S(1)}, f32[48,2,2,16,1]{0,3,4,2,1:T(8,128)S(1)}, u32[]{:S(2)}, u32[]{:S(2)}) collective-permute-start(f32[48,2,2,16,1]{0,3,4,2,1:T(8,128)S(1)} %copy.28), channel_id=1, source_target_pairs={{0,1},{1,2},{2,3},{4,5},{5,6},{6,7},{8,9},{9,10},{10,11},{12,13},{... | collective-permute-start | bytes 36872 | tf_op jit(solution)/shard_map/ppermute | solution.py:18
  225.5 2.4 fusion.7
  228.0 2.4 copy.27
  230.3 2.4 copy.29
  232.7 4.3 %fusion.8 = f32[48,2,2,16,256]{4,3,2,1,0:T(8,128)S(1)} fusion(f32[48,2,2,16,1]{4,3,2,1,0:T(8,128)} %copy.27, f32[48,2,2,16,255]{4,3,2,1,0:T(8,128)} %get-tuple-element.74, f32[48,2,2,16,255]{4,3,2,1,0:T(8,128)S(1)} %copy-done.2, f32[48,2,2,16,1]{4,3,2,1,0:T(8,128)} %copy.29, f32[16,256]{1,0:T(8,128)S(1)} %broadcast_divide_fusion.1), kind=kLoop, calls=%fused_computation.15 | loop fusion | flops 3145728 | bytes 9453568 | tf_op jit(solution)/shard_map/mul | solution.py:84
  237.4 2.1 fusion.44
  239.5 22.3 %psum.7 = f32[2,16,256]{2,1,0:T(8,128)S(1)} all-reduce(f32[2,16,256]{2,1,0:T(8,128)S(1)} %get-tuple-element.67), channel_id=1, replica_groups=mesh['tm'=8,'tile'=4] {'tm'}, use_global_device_ids=true, to_apply=%region_3.5 | all-reduce | flops 8192 | bytes 65536 | tf_op jit(solution)/shard_map/psum | solution.py:95
  (39 shorter events, 7.6 us)
Async XLA Ops:
  0.6 2.7 %copy-start.3 = (f32[48,2,16,256]{3,2,1,0:T(8,128)S(1)}, f32[48,2,16,256]{3,2,1,0:T(8,128)}, u32[]{:S(2)}) copy-start(f32[48,2,16,256]{3,2,1,0:T(8,128)} %param.10) | copy-start | bytes 4718596
  31.0 43.1 %all-to-all-start = ((f32[8,1,98304]{2,1,0:T(1,128)}), f32[8,1,98304]{2,1,0:T(1,128)S(1)}, u32[]{:S(2)}, u32[]{:S(2)}) async-start(f32[8,1,98304]{2,1,0:T(1,128)} %reshape.50), calls=%async_computation | async-start | bytes 6291456 | tf_op jit(solution)/shard_map/all_to_all | solution.py:71
  156.2 4.0 %copy-start.5 = (s32[16,256]{1,0:T(8,128)S(1)}, s32[16,256]{1,0:T(8,128)}, u32[]{:S(2)}) copy-start(s32[16,256]{1,0:T(8,128)} %param.11) | copy-start | bytes 49156
  156.2 4.0 %copy-start.6 = (f32[16,256]{1,0:T(8,128)S(1)}, f32[16,256]{1,0:T(8,128)}, u32[]{:S(2)}) copy-start(f32[16,256]{1,0:T(8,128)} %param.13) | copy-start | bytes 49156
  156.2 4.0 %copy-start.7 = (f32[16,256]{1,0:T(8,128)S(1)}, f32[16,256]{1,0:T(8,128)}, u32[]{:S(2)}) copy-start(f32[16,256]{1,0:T(8,128)} %param.14) | copy-start | bytes 49156
  156.2 4.1 %copy-start.4 = (s32[16,256]{1,0:T(8,128)S(1)}, s32[16,256]{1,0:T(8,128)}, u32[]{:S(2)}) copy-start(s32[16,256]{1,0:T(8,128)} %param.12) | copy-start | bytes 49156
  156.2 41.8 %all-to-all-start.1 = ((f32[384,2,1024]{2,1,0:T(2,128)}), f32[384,2,1024]{2,1,0:T(2,128)S(1)}, u32[]{:S(2)}, u32[]{:S(2)}) async-start(f32[384,2,1024]{2,1,0:T(2,128)} %reshape_reshape.3), calls=%async_computation.1 | async-start | bytes 6291456 | tf_op jit(solution)/shard_map/all_to_all | solution.py:73
  217.3 10.7 %collective-permute-start = (f32[48,2,2,16,1]{0,3,4,2,1:T(8,128)S(1)}, f32[48,2,2,16,1]{0,3,4,2,1:T(8,128)S(1)}, u32[]{:S(2)}, u32[]{:S(2)}) collective-permute-start(f32[48,2,2,16,1]{0,3,4,2,1:T(8,128)S(1)} %copy.26), channel_id=1, source_target_pairs={{1,0},{2,1},{3,2},{5,4},{6,5},{7,6},{9,8},{10,9},{11,10},{13,12},{... | collective-permute-start | bytes 36872 | tf_op jit(solution)/shard_map/ppermute | solution.py:19
  220.8 9.6 %collective-permute-start.1 = (f32[48,2,2,16,1]{0,3,4,2,1:T(8,128)S(1)}, f32[48,2,2,16,1]{0,3,4,2,1:T(8,128)S(1)}, u32[]{:S(2)}, u32[]{:S(2)}) collective-permute-start(f32[48,2,2,16,1]{0,3,4,2,1:T(8,128)S(1)} %copy.28), channel_id=1, source_target_pairs={{0,1},{1,2},{2,3},{4,5},{5,6},{6,7},{8,9},{9,10},{10,11},{12,13},{... | collective-permute-start | bytes 36872 | tf_op jit(solution)/shard_map/ppermute | solution.py:18
  228.0 4.7 %copy-start.2 = (f32[48,2,2,16,255]{4,3,2,1,0:T(8,128)S(1)}, f32[48,2,2,16,255]{4,3,2,1,0:T(8,128)}, u32[]{:S(2)}) copy-start(f32[48,2,2,16,255]{4,3,2,1,0:T(8,128)} %get-tuple-element.73) | copy-start | bytes 9400324
  232.7 4.3 %copy-start = (f32[48,2,2,16,256]{4,3,2,1,0:T(8,128)S(1)}, f32[48,2,2,16,256]{4,3,2,1,0:T(8,128)}, u32[]{:S(2)}) copy-start(f32[48,2,2,16,256]{4,3,2,1,0:T(8,128)} %fusion.7) | copy-start | bytes 9437188
  232.7 4.7 %copy-start.1 = (f32[48,2,2,16,256]{4,3,2,1,0:T(8,128)S(1)}, f32[48,2,2,16,256]{4,3,2,1,0:T(8,128)}, u32[]{:S(2)}) copy-start(f32[48,2,2,16,256]{4,3,2,1,0:T(8,128)} %get-tuple-element.69) | copy-start | bytes 9437188
where the time goes:
time: 267 us; the launch traced here: 263 us
  local copies, waits for them, and re-layouts  90.8 us (34%)
  waiting for transfers between devices  74.5 us (28%)
  other arithmetic  29.2 us (11%)
  matrix products  24.2 us (9%)
  blocking collectives  22.3 us (8%)
  starting transfers between devices  15.4 us (6%)
  loops' own time  5.18 us (2%)
    all_to_all x1, waiting for transfers between devices, shards(): lax.all_to_all(series_mean, 'tm', split_axis=0, concat_axis=2, tiled=True)  37.7 us
    unnamed x19, local copies, waits for them, and re-layouts  37.3 us
    all_to_all x1, waiting for transfers between devices, shards(): lax.all_to_all(flat_cells, 'tm', split_axis=2, concat_axis=0, tiled=True)  36.8 us
    psum x1, blocking collectives, shards(): summed = lax.psum(jnp.sum(conversion, axis=0), 'tm')  22.3 us
    dot_general x8, matrix products, one_block(): jnp.dot(matrix, window, precision=lax.Precision.HIGHEST, preferred_elemen...  16.8 us
    another operation x3, local copies, waits for them, and re-layouts, shards(): stacked = jnp.stack([velocity_u, velocity_v], axis=1)  12.1 us
    all_to_all x1, other arithmetic, shards(): lax.all_to_all(flat_cells, 'tm', split_axis=2, concat_axis=0, tiled=True)  11.2 us
    all_to_all x3, local copies, waits for them, and re-layouts, shards(): lax.all_to_all(flat_cells, 'tm', split_axis=2, concat_axis=0, tiled=True)  9.91 us
  transfers between devices with their start and end apart: 4, of which 2 were waited for; matrix products, arithmetic and copies ran while one was open for 3% of the time, Pallas kernels for 0%

commit v1 on v0

--- a/solution.py
+++ b/solution.py
@@ -92,7 +92,7 @@
         + eddy_v * eddy_v * grad_y[:, 1]
     )
     conversion = -wet_mask[None] * total
-    summed = lax.psum(jnp.sum(conversion, axis=0), "tm")
+    summed = jnp.sum(lax.all_gather(jnp.sum(conversion, axis=0), "tm"), axis=0)
     return (conversion.astype(jnp.bfloat16), summed / total_len)
 
 

time: 267 us -> 253 us (0.948)
  blocking collectives: 22.3 us -> 8.32 us
    psum x1 -> x0, blocking collectives: 22.3 us -> none  [shards(): summed = lax.psum(jnp.sum(conversion, axis=0), 'tm')]
    all_gather x0 -> x1, blocking collectives: none -> 8.32 us  [shards(): summed = jnp.sum(lax.all_gather(jnp.sum(conversion, axis=0), 'tm'), axis=0)]
where the time goes in v1:
time: 253 us; the launch traced here: 249 us
  local copies, waits for them, and re-layouts  90.8 us (36%)
  waiting for transfers between devices  74.5 us (29%)
  other arithmetic  29.2 us (12%)
  matrix products  24.2 us (10%)
  starting transfers between devices  15.4 us (6%)
  blocking collectives  8.32 us (3%)
  loops' own time  5.18 us (2%)
    all_to_all x1, waiting for transfers between devices, shards(): lax.all_to_all(series_mean, 'tm', split_axis=0, concat_axis=2, tiled=True)  37.7 us
    unnamed x19, local copies, waits for them, and re-layouts  37.3 us
    all_to_all x1, waiting for transfers between devices, shards(): lax.all_to_all(flat_cells, 'tm', split_axis=2, concat_axis=0, tiled=True)  36.8 us
    dot_general x8, matrix products, one_block(): jnp.dot(matrix, window, precision=lax.Precision.HIGHEST, preferred_elemen...  16.8 us
    another operation x3, local copies, waits for them, and re-layouts, shards(): stacked = jnp.stack([velocity_u, velocity_v], axis=1)  12.1 us
    all_to_all x1, other arithmetic, shards(): lax.all_to_all(flat_cells, 'tm', split_axis=2, concat_axis=0, tiled=True)  11.2 us
    all_to_all x3, local copies, waits for them, and re-layouts, shards(): lax.all_to_all(flat_cells, 'tm', split_axis=2, concat_axis=0, tiled=True)  9.91 us
    all_gather x1, blocking collectives, shards(): summed = jnp.sum(lax.all_gather(jnp.sum(conversion, axis=0), 'tm'), axis=0)  8.32 us
  transfers between devices with their start and end apart: 4, of which 2 were waited for; matrix products, arithmetic and copies ran while one was open for 3% of the time, Pallas kernels for 0%

profile of v1, /device:TPU:0, one launch (start us, length us, event | category | flops | bytes accessed | tf_op | source)
XLA Modules:
  0.0 248.7 jit_solution(3495436349109585962)
XLA Ops:
  0.6 2.7 %stack.18 = f32[48,1,8192]{2,0,1:T(8,128)} reshape(f32[48,2,16,256]{3,2,1,0:T(8,128)} %param.9) | data formatting | bytes 3145728 | tf_op jit(solution)/shard_map/stack | solution.py:67
  3.3 1.4 stack.19
  4.8 2.1 pad_maximum_fusion
  6.9 8.0 %copy.21 = f32[48,2,8192]{0,1,2:T(2,128)} copy(f32[48,2,8192]{2,0,1:T(8,128)S(1)} %pad_maximum_fusion) | data formatting | bytes 6291456 | tf_op jit(solution)/shard_map/stack | solution.py:67
  14.9 16.2 %reshape.51 = f32[8,1,98304]{2,1,0:T(1,128)} reshape(f32[8192,2,48]{2,1,0:T(2,128)} %bitcast.50) | data formatting | bytes 6291456
  31.0 5.4 %all-to-all-start = ((f32[8,1,98304]{2,1,0:T(1,128)}), f32[8,1,98304]{2,1,0:T(1,128)S(1)}, u32[]{:S(2)}, u32[]{:S(2)}) async-start(f32[8,1,98304]{2,1,0:T(1,128)} %reshape.51), calls=%async_computation | async-start | bytes 6291456 | tf_op jit(solution)/shard_map/all_to_all | solution.py:71
  37.2 36.8 %all-to-all-done = f32[8,1,98304]{2,1,0:T(1,128)S(1)} async-done(((f32[8,1,98304]{2,1,0:T(1,128)}), f32[8,1,98304]{2,1,0:T(1,128)S(1)}, u32[]{:S(2)}, u32[]{:S(2)}) %all-to-all-start) | async-done | bytes 3145760 | tf_op jit(solution)/shard_map/all_to_all | solution.py:71
  74.6 11.2 %reduce = f32[8,98304]{1,0:T(8,128)} reduce(f32[8,1,98304]{2,1,0:T(1,128)S(1)} %all-to-all-done, f32[]{:T(128)} %broadcast.65), dimensions={1}, to_apply=%all_to_all.22.reduce_sub_computation | reduce | bytes 6291460 | tf_op jit(solution)/shard_map/all_to_all | solution.py:71
  85.8 19.3 %reshape.52 = f32[8192,2,48]{2,1,0:T(2,128)} reshape(f32[8,98304]{1,0:T(8,128)} %reduce) | data formatting | bytes 6291456
  105.1 7.0 %copy.30 = f32[48,2,8,1024]{3,2,0,1:T(8,128)S(1)} copy(f32[48,2,8,1024]{0,1,3,2:T(2,128)} %bitcast.51) | data formatting | bytes 6291456 | tf_op jit(solution)/shard_map/all_to_all | solution.py:71
  112.1 2.4 copy.23
  114.5 1.4 copy.31
  116.3 34.3 %while.11 = (s32[]{:T(128)}, f32[8,48,2048]{2,1,0:T(8,128)}, s32[8]{0:T(128)S(1)}, f32[432,2048]{1,0:T(8,128)S(1)}, f32[48,96]{1,0:T(8,128)}, /*index=5*/f32[432...) while((s32[]{:T(128)}, f32[8,48,2048]{2,1,0:T(8,128)}, s32[8]{0:T(128)S(1)}, ...), condition=%wide.region_1.3_spmd.clone, body=%wide.region_0.2_spmd.clone.sunk | while | flops 113399816 | bytes 1224551 | solution.py:47
  117.6 0.9 convolution_bitcast_fusion.2
  118.5 2.1 fusion.59
  121.9 0.9 convolution_bitcast_fusion.2
  122.9 2.1 fusion.59
  126.2 0.9 convolution_bitcast_fusion.2
  127.1 2.1 fusion.59
  130.5 0.9 convolution_bitcast_fusion.2
  131.4 2.1 fusion.59
  134.8 0.9 convolution_bitcast_fusion.2
  135.7 2.1 fusion.59
  139.0 0.9 convolution_bitcast_fusion.2
  140.0 2.1 fusion.59
  143.3 0.9 convolution_bitcast_fusion.2
  144.3 2.1 fusion.59
  147.6 0.9 convolution_bitcast_fusion.2
  148.5 2.1 fusion.59
  150.6 5.6 %reshape_reshape.3 = f32[384,2,1024]{2,1,0:T(2,128)} reshape(f32[8,48,2048]{2,1,0:T(8,128)} %get-tuple-element.38) | data formatting | bytes 6291456 | tf_op jit(solution)/shard_map/reshape;reshape | solution.py:61
  156.2 4.0 %all-to-all-start.1 = ((f32[384,2,1024]{2,1,0:T(2,128)}), f32[384,2,1024]{2,1,0:T(2,128)S(1)}, u32[]{:S(2)}, u32[]{:S(2)}) async-start(f32[384,2,1024]{2,1,0:T(2,128)} %reshape_reshape.3), calls=%async_computation.1 | async-start | bytes 6291456 | tf_op jit(solution)/shard_map/all_to_all | solution.py:73
  160.3 37.7 %all-to-all-done.1 = f32[384,2,1024]{2,1,0:T(2,128)S(1)} async-done(((f32[384,2,1024]{2,1,0:T(2,128)}), f32[384,2,1024]{2,1,0:T(2,128)S(1)}, u32[]{:S(2)}, u32[]{:S(2)}) %all-to-all-start.1) | async-done | bytes 3145760 | tf_op jit(solution)/shard_map/all_to_all | solution.py:73
  198.0 1.0 copy.24
  199.0 1.8 copy.25
  200.8 2.6 %reshape.47 = f32[48,2,2,16,256]{4,3,2,1,0:T(8,128)} reshape(f32[48,2,8,1024]{3,2,1,0:T(8,128)S(1)} %copy.25) | data formatting | bytes 6291456 | tf_op jit(solution)/shard_map/reshape | solution.py:74
  203.4 5.7 %maximum_subtract_fusion = (f32[48,2,2,16,256]{4,3,2,1,0:T(8,128)}, f32[48,2,2,16,256]{4,3,2,1,0:T(8,128)S(1)}) fusion(f32[48,2,2,16,256]{4,3,2,1,0:T(8,128)} %reshape.47, f32[48,1,2,16,256]{4,3,2,1,0:T(8,128)} %bitcast.56, f32[48,1,2,16,256]{4,3,2,1,0:T(8,128)} %bitcast.57, f32[2,16,256]{2,1,0:T(8,128)S(1)} %fusion.15), kind=kLoop, calls=%fused_computation.12 | loop fusion | flops 2359296 | bytes 12615680 | tf_op jit(solution)/shard_map/sub | solution.py:75
  209.1 3.7 %fusion.47 = (f32[48,2,2,16,255]{4,3,2,1,0:T(8,128)}, f32[48,2,2,16,255]{4,3,2,1,0:T(8,128)}) fusion(f32[48,2,2,16,256]{4,3,2,1,0:T(8,128)S(1)} %get-tuple-element.70), kind=kLoop, calls=%fused_computation.85 | loop fusion | bytes 12533760 | tf_op jit(solution)/shard_map/slice | solution.py:83
  212.8 2.3 fusion.46
  215.1 2.2 copy.26
  217.3 1.3 collective-permute-start
  218.6 2.2 copy.28
  220.8 4.7 %collective-permute-start.1 = (f32[48,2,2,16,1]{0,3,4,2,1:T(8,128)S(1)}, f32[48,2,2,16,1]{0,3,4,2,1:T(8,128)S(1)}, u32[]{:S(2)}, u32[]{:S(2)}) collective-permute-start(f32[48,2,2,16,1]{0,3,4,2,1:T(8,128)S(1)} %copy.28), channel_id=1, source_target_pairs={{0,1},{1,2},{2,3},{4,5},{5,6},{6,7},{8,9},{9,10},{10,11},{12,13},{... | collective-permute-start | bytes 36872 | tf_op jit(solution)/shard_map/ppermute | solution.py:18
  225.5 2.4 fusion.7
  228.0 2.4 copy.27
  230.3 2.4 copy.29
  232.7 4.3 %fusion.8 = f32[48,2,2,16,256]{4,3,2,1,0:T(8,128)S(1)} fusion(f32[48,2,2,16,1]{4,3,2,1,0:T(8,128)} %copy.27, f32[48,2,2,16,255]{4,3,2,1,0:T(8,128)} %get-tuple-element.74, f32[48,2,2,16,255]{4,3,2,1,0:T(8,128)S(1)} %copy-done.2, f32[48,2,2,16,1]{4,3,2,1,0:T(8,128)} %copy.29, f32[16,256]{1,0:T(8,128)S(1)} %broadcast_divide_fusion.1), kind=kLoop, calls=%fused_computation.15 | loop fusion | flops 3145728 | bytes 9453568 | tf_op jit(solution)/shard_map/mul | solution.py:84
  237.4 2.1 fusion.44
  239.5 8.3 %all-gather = f32[16,16,256]{2,1,0:T(8,128)S(1)} all-gather(f32[2,16,256]{2,1,0:T(8,128)S(1)} %get-tuple-element.67), channel_id=2, replica_groups=mesh['tm'=8,'tile'=4] {'tm'}, dimensions={0}, use_global_device_ids=true | all-gather | bytes 294912 | tf_op jit(solution)/shard_map/all_gather | solution.py:95
  (40 shorter events, 7.6 us)
Async XLA Ops:
  0.6 2.7 %copy-start.3 = (f32[48,2,16,256]{3,2,1,0:T(8,128)S(1)}, f32[48,2,16,256]{3,2,1,0:T(8,128)}, u32[]{:S(2)}) copy-start(f32[48,2,16,256]{3,2,1,0:T(8,128)} %param.10) | copy-start | bytes 4718596
  31.0 43.1 %all-to-all-start = ((f32[8,1,98304]{2,1,0:T(1,128)}), f32[8,1,98304]{2,1,0:T(1,128)S(1)}, u32[]{:S(2)}, u32[]{:S(2)}) async-start(f32[8,1,98304]{2,1,0:T(1,128)} %reshape.51), calls=%async_computation | async-start | bytes 6291456 | tf_op jit(solution)/shard_map/all_to_all | solution.py:71
  156.2 4.0 %copy-start.5 = (s32[16,256]{1,0:T(8,128)S(1)}, s32[16,256]{1,0:T(8,128)}, u32[]{:S(2)}) copy-start(s32[16,256]{1,0:T(8,128)} %param.11) | copy-start | bytes 49156
  156.2 4.0 %copy-start.6 = (f32[16,256]{1,0:T(8,128)S(1)}, f32[16,256]{1,0:T(8,128)}, u32[]{:S(2)}) copy-start(f32[16,256]{1,0:T(8,128)} %param.13) | copy-start | bytes 49156
  156.2 4.0 %copy-start.7 = (f32[16,256]{1,0:T(8,128)S(1)}, f32[16,256]{1,0:T(8,128)}, u32[]{:S(2)}) copy-start(f32[16,256]{1,0:T(8,128)} %param.14) | copy-start | bytes 49156
  156.2 4.1 %copy-start.4 = (s32[16,256]{1,0:T(8,128)S(1)}, s32[16,256]{1,0:T(8,128)}, u32[]{:S(2)}) copy-start(s32[16,256]{1,0:T(8,128)} %param.12) | copy-start | bytes 49156
  156.2 41.8 %all-to-all-start.1 = ((f32[384,2,1024]{2,1,0:T(2,128)}), f32[384,2,1024]{2,1,0:T(2,128)S(1)}, u32[]{:S(2)}, u32[]{:S(2)}) async-start(f32[384,2,1024]{2,1,0:T(2,128)} %reshape_reshape.3), calls=%async_computation.1 | async-start | bytes 6291456 | tf_op jit(solution)/shard_map/all_to_all | solution.py:73
  217.3 10.7 %collective-permute-start = (f32[48,2,2,16,1]{0,3,4,2,1:T(8,128)S(1)}, f32[48,2,2,16,1]{0,3,4,2,1:T(8,128)S(1)}, u32[]{:S(2)}, u32[]{:S(2)}) collective-permute-start(f32[48,2,2,16,1]{0,3,4,2,1:T(8,128)S(1)} %copy.26), channel_id=1, source_target_pairs={{1,0},{2,1},{3,2},{5,4},{6,5},{7,6},{9,8},{10,9},{11,10},{13,12},{... | collective-permute-start | bytes 36872 | tf_op jit(solution)/shard_map/ppermute | solution.py:19
  220.8 9.6 %collective-permute-start.1 = (f32[48,2,2,16,1]{0,3,4,2,1:T(8,128)S(1)}, f32[48,2,2,16,1]{0,3,4,2,1:T(8,128)S(1)}, u32[]{:S(2)}, u32[]{:S(2)}) collective-permute-start(f32[48,2,2,16,1]{0,3,4,2,1:T(8,128)S(1)} %copy.28), channel_id=1, source_target_pairs={{0,1},{1,2},{2,3},{4,5},{5,6},{6,7},{8,9},{9,10},{10,11},{12,13},{... | collective-permute-start | bytes 36872 | tf_op jit(solution)/shard_map/ppermute | solution.py:18
  228.0 4.7 %copy-start.2 = (f32[48,2,2,16,255]{4,3,2,1,0:T(8,128)S(1)}, f32[48,2,2,16,255]{4,3,2,1,0:T(8,128)}, u32[]{:S(2)}) copy-start(f32[48,2,2,16,255]{4,3,2,1,0:T(8,128)} %get-tuple-element.73) | copy-start | bytes 9400324
  232.7 4.3 %copy-start = (f32[48,2,2,16,256]{4,3,2,1,0:T(8,128)S(1)}, f32[48,2,2,16,256]{4,3,2,1,0:T(8,128)}, u32[]{:S(2)}) copy-start(f32[48,2,2,16,256]{4,3,2,1,0:T(8,128)} %fusion.7) | copy-start | bytes 9437188
  232.7 4.7 %copy-start.1 = (f32[48,2,2,16,256]{4,3,2,1,0:T(8,128)S(1)}, f32[48,2,2,16,256]{4,3,2,1,0:T(8,128)}, u32[]{:S(2)}) copy-start(f32[48,2,2,16,256]{4,3,2,1,0:T(8,128)} %get-tuple-element.69) | copy-start | bytes 9437188
